TPU v7x, 256 devices: a whole 4x4x8 slice. The times are simulated.
256 devices in a mesh: blk: 64 (over z, x, core), grp: 4 (over y).
Axes of the slice: x: 4, y: 4, z: 8, core: 2. Of those that a mesh axis runs over, the one named last changes fastest.
Arguments:
- features: bfloat16 [131072, 128], P(('blk', 'grp')), may hold values from -6 to 6
- weight: bfloat16 [128, 256], replicated, may hold values from -0.5 to 0.5
- cotangent: bfloat16 [131072, 256], P(('blk', 'grp')), may hold values from -6 to 6
- tiles: bfloat16 [16384, 128, 128], P(('blk', 'grp')), may hold values from -0.125 to 0.125
- tile_row: int32 [16384], P(('blk', 'grp')), may hold values from 0 to 3
- tile_col: int32 [16384], P(('blk', 'grp')), may hold values from 0 to 23
- hub_index: int32 [32768], P(('blk', 'grp')), may hold values from 0 to 511
- send_index: int32 [16384, 32], P(('blk', 'grp')), may hold values from 0 to 511
- send_count: int32 [16384], P(('blk', 'grp')), may hold values from 1 to 32, as said below
Outputs:
- activations: bfloat16 [131072, 256], P(('blk', 'grp'))
- weight_grad: float32 [128, 256], replicated
- feature_grad: float32 [131072, 128], P(('blk', 'grp'))
Inputs may be any that keep to these rules, and one draw needn't show every extreme that they name: `send_count`: each device has at least one destination whose count is 32.
All inputs are finite; a program needn't handle non-finite values.
Results may differ from a plain program's by a relative error of at most 0.0085.
Values may be sent and summed in bfloat16 or wider, within the bound.
A program may use at most 64 MiB of HBM per device.

v0:
```python
import jax
import jax.numpy as jnp
from jax import lax
from jax.sharding import PartitionSpec as P


def silu_grad(values):
    logistic = jax.nn.sigmoid(values)
    return logistic * (1.0 + values * (1.0 - logistic))


def body(features, weight, cotangent, tiles, tile_row, tile_col, hub_index, send_index, send_count):
    row_count, width_in = features.shape
    width_out = weight.shape[1]
    tile_size = tiles.shape[1]
    block_count, slot_count = send_index.shape
    row_tiles = row_count // tile_size
    slot_live = lax.broadcasted_iota(jnp.int32, send_index.shape, 1) < send_count[:, None]
    outgoing = jnp.where(slot_live[:, :, None], features[send_index], jnp.zeros((), features.dtype))
    incoming = lax.all_to_all(outgoing, "blk", split_axis=0, concat_axis=0, tiled=True)
    hub_table = lax.all_gather(features[hub_index], "grp", axis=0, tiled=True)
    sources = jnp.concatenate(
        [features, incoming.reshape(block_count * slot_count, width_in), hub_table], axis=0
    )
    source_tiles = sources.shape[0] // tile_size
    sources = sources.reshape(source_tiles, tile_size, width_in)
    products = jnp.einsum(
        "lij,ljf->lif", tiles, sources[tile_col], preferred_element_type=jnp.float32
    )
    summed_rows = (
        jnp.zeros((row_tiles, tile_size, width_in), jnp.float32).at[tile_row].add(products)
    )
    aggregated = summed_rows.reshape(row_count, width_in).astype(jnp.bfloat16)
    preact = jnp.dot(aggregated, weight, preferred_element_type=jnp.float32)
    activations = jax.nn.silu(preact).astype(jnp.bfloat16)
    pre_grad = (cotangent.astype(jnp.float32) * silu_grad(preact)).astype(jnp.bfloat16)
    weight_part = lax.dot_general(
        aggregated, pre_grad, (((0,), (0,)), ((), ())), preferred_element_type=jnp.float32
    )
    backward = jnp.einsum(
        "lij,lif->ljf",
        tiles,
        pre_grad.reshape(row_tiles, tile_size, width_out)[tile_row],
        preferred_element_type=jnp.float32,
    )
    source_grad = (
        jnp.zeros((source_tiles, tile_size, width_out), jnp.float32).at[tile_col].add(backward)
    )
    source_grad = source_grad.reshape(source_tiles * tile_size, width_out)
    weight_wide = weight.astype(jnp.float32)
    grad_width = source_grad.shape[1]
    boundary_end = row_count + block_count * slot_count
    returned = lax.all_to_all(
        source_grad[row_count:boundary_end]
        .reshape(block_count, slot_count, grad_width)
        .astype(jnp.bfloat16),
        "blk",
        split_axis=0,
        concat_axis=0,
        tiled=True,
    ).astype(jnp.float32)
    hub_part = source_grad[boundary_end:]
    own_hubs = lax.psum_scatter(
        hub_part.astype(jnp.bfloat16), "grp", scatter_dimension=0, tiled=True
    ).astype(jnp.float32)
    weight_grad = lax.psum(weight_part, ("blk", "grp"))
    returned = jnp.where(slot_live[:, :, None], returned, jnp.zeros((), returned.dtype))
    feature_grad = (
        source_grad[:row_count].at[send_index.reshape(-1)].add(returned.reshape(-1, grad_width))
    )
    feature_grad = feature_grad.at[hub_index].add(own_hubs)
    feature_grad = lax.dot_general(
        feature_grad, weight_wide, (((1,), (1,)), ((), ())), precision=lax.Precision.HIGHEST
    )
    return (activations, weight_grad, feature_grad)


def solution(mesh):
    return jax.shard_map(
        body,
        mesh=mesh,
        in_specs=(
            P(("blk", "grp"), None),
            P(),
            P(("blk", "grp"), None),
            P(("blk", "grp"), None, None),
            P(("blk", "grp")),
            P(("blk", "grp")),
            P(("blk", "grp")),
            P(("blk", "grp"), None),
            P(("blk", "grp")),
        ),
        out_specs=(P(("blk", "grp"), None), P(), P(("blk", "grp"), None)),
        check_vma=False,
    )
```

profile of v0, /device:TPU:1, one launch (start us, length us, event | category | flops | bytes accessed | tf_op | source)
XLA Modules:
  0.0 382.7 jit_solution(15053770784025251206)
XLA Ops:
  9.8 6.2 %gather_fusion = bf16[2048,128]{1,0:T(8,128)(2,1)S(1)} fusion(bf16[512,128]{1,0:T(8,128)(2,1)S(1)} %copy-done.1, s32[2048]{0:T(1024)S(1)} %broadcast_clamp_fusion), kind=kCustom, calls=%fused_computation | custom fusion | bytes 1056768 | tf_op jit(solution)/shard_map/gather | solution.py:19
  16.1 1.1 broadcast_select_fusion
  17.2 13.0 %all-to-all-start = ((bf16[64,32,128]{2,1,0:T(8,128)(2,1)}), bf16[64,32,128]{2,1,0:T(8,128)(2,1)S(1)}, u32[]{:S(2)}, u32[]{:S(2)}) async-start(bf16[64,32,128]{2,1,0:T(8,128)(2,1)} %broadcast_select_fusion), calls=%async_computation | async-start | bytes 1048576 | tf_op jit(solution)/shard_map/all_to_all | solution.py:20
  31.5 10.9 %all-gather = bf16[512,128]{1,0:T(8,128)(2,1)} all-gather(bf16[128,128]{1,0:T(8,128)(2,1)S(1)} %gather_fusion.1), channel_id=2, replica_groups=mesh['blk'=64,'grp'=4] {'grp'}, dimensions={0}, use_global_device_ids=true | all-gather | bytes 163840 | tf_op jit(solution)/shard_map/all_gather | solution.py:21
  43.0 4.9 %all-to-all-done = bf16[64,32,128]{2,1,0:T(8,128)(2,1)S(1)} async-done(((bf16[64,32,128]{2,1,0:T(8,128)(2,1)}), bf16[64,32,128]{2,1,0:T(8,128)(2,1)S(1)}, u32[]{:S(2)}, u32[]{:S(2)}) %all-to-all-start) | async-done | bytes 524320 | tf_op jit(solution)/shard_map/all_to_all | solution.py:20
  48.9 2.1 gather_fusion.2
  51.0 5.1 %convolution_bitcast_fusion.1 = f32[64,128,128]{1,2,0:T(8,128)} fusion(bf16[64,128,128]{2,1,0:T(8,128)(2,1)} %gather_fusion.2, bf16[64,128,128]{2,1,0:T(8,128)(2,1)S(1)} %copy-done), kind=kOutput, calls=%fused_computation.9 | convolution fusion | flops 268435456 | bytes 8388608 | tf_op jit(solution)/shard_map/lij,ljf->lif/dot_general | solution.py:27
  56.1 5.6 %copy.16 = f32[64,128,128]{2,1,0:T(8,128)} copy(f32[64,128,128]{1,2,0:T(8,128)} %convolution_bitcast_fusion.1) | data formatting | bytes 8388608 | tf_op jit(solution)/shard_map/lij,ljf->lif/dot_general | solution.py:27
  61.8 8.8 %scatter_fusion = f32[4,128,128]{2,1,0:T(8,128)S(1)} fusion(f32[4,128,128]{2,1,0:T(8,128)S(1)} %broadcast_in_dim.49, s32[64]{0:T(128)S(1)} %copy-done.8, f32[64,128,128]{2,1,0:T(8,128)} %copy.16), kind=kCustom, calls=%fused_computation.4 | custom fusion | flops 1048576 | bytes 12583168 | tf_op jit(solution)/shard_map/scatter-add | solution.py:31
  71.8 2.8 gather_fusion.3
  74.5 6.7 %convolution_bitcast_fusion = f32[64,128,256]{1,2,0:T(8,128)} fusion(bf16[64,128,256]{2,1,0:T(8,128)(2,1)} %gather_fusion.3, bf16[64,128,128]{2,1,0:T(8,128)(2,1)S(1)} %copy-done), kind=kOutput, calls=%fused_computation.8 | convolution fusion | flops 536870912 | bytes 14680064 | tf_op jit(solution)/shard_map/lij,lif->ljf/dot_general | solution.py:40
  81.2 9.0 %copy.18 = f32[64,128,256]{2,1,0:T(8,128)} copy(f32[64,128,256]{1,2,0:T(8,128)} %convolution_bitcast_fusion) | data formatting | bytes 16777216 | tf_op jit(solution)/shard_map/lij,lif->ljf/dot_general | solution.py:40
  90.2 2.1 broadcast_in_dim.56
  92.3 19.2 %scatter_fusion.1 = f32[24,128,256]{2,1,0:T(8,128)} fusion(f32[24,128,256]{2,1,0:T(8,128)} %broadcast_in_dim.56, s32[64]{0:T(128)S(1)} %copy-done.6, f32[64,128,256]{2,1,0:T(8,128)} %copy.18), kind=kCustom, calls=%fused_computation.5 | custom fusion | flops 2097152 | bytes 25166080 | tf_op jit(solution)/shard_map/scatter-add | solution.py:47
  111.5 2.1 convert.4
  113.6 1.1 copy-done.2
  115.8 8.3 %all-to-all-start.1 = ((bf16[64,32,256]{2,1,0:T(8,128)(2,1)}), bf16[64,32,256]{2,1,0:T(8,128)(2,1)}, u32[]{:S(2)}, u32[]{:S(2)}) async-start(bf16[64,32,256]{2,1,0:T(8,128)(2,1)} %bitcast.9), calls=%async_computation.1 | async-start | bytes 2097152 | tf_op jit(solution)/shard_map/all_to_all | solution.py:53
  124.4 1.7 slice.30
  128.1 24.0 %all-to-all-done.1 = bf16[64,32,256]{2,1,0:T(8,128)(2,1)} async-done(((bf16[64,32,256]{2,1,0:T(8,128)(2,1)}), bf16[64,32,256]{2,1,0:T(8,128)(2,1)}, u32[]{:S(2)}, u32[]{:S(2)}) %all-to-all-start.1) | async-done | bytes 1048608 | tf_op jit(solution)/shard_map/all_to_all | solution.py:53
  152.1 2.9 convert_select_fusion
  155.0 12.4 %scatter_fusion.2 = f32[512,256]{1,0:T(8,128)S(1)} fusion(f32[512,256]{1,0:T(8,128)S(1)} %bitcast.24, s32[2048]{0:T(1024)S(1)} %bitcast.33, f32[2048,256]{1,0:T(8,128)} %bitcast.27), kind=kCustom, calls=%fused_computation.6 | custom fusion | flops 524288 | bytes 6299648 | tf_op jit(solution)/shard_map/scatter-add | solution.py:69
  167.4 1.8 scatter_custom_fusion.3
  170.3 203.4 %all-reduce.2.cloned.1.call-done = f32[128,256]{1,0:T(8,128)} async-done(((f32[128,256]{1,0:T(8,128)}), f32[128,256]{1,0:T(8,128)}) %all-reduce.2.cloned.1.call-update) | async-done | bytes 131088 | tf_op jit(solution)/shard_map/psum | solution.py:66
  373.7 1.6 copy.27
  (55 shorter events, 10.2 us)
Async XLA Ops:
  8.0 43.0 %copy-start = (bf16[64,128,128]{2,1,0:T(8,128)(2,1)S(1)}, bf16[64,128,128]{2,1,0:T(8,128)(2,1)}, u32[]{:S(2)}) copy-start(bf16[64,128,128]{2,1,0:T(8,128)(2,1)} %param.12) | copy-start | bytes 6291460
  8.0 1.8 copy-start.1
  16.0 14.2 %copy-start.11 = (s32[128]{0:T(128)S(1)}, s32[128]{0:T(128)}, u32[]{:S(2)}) copy-start(s32[128]{0:T(128)} %param.15) | copy-start | bytes 1540
  16.0 26.4 %copy-start.12 = (s32[64]{0:T(128)S(1)}, s32[64]{0:T(128)}, u32[]{:S(2)}) copy-start(s32[64]{0:T(128)} %param.14) | copy-start | bytes 772
  16.0 26.9 %copy-start.13 = (s32[64]{0:T(128)S(1)}, s32[64]{0:T(128)}, u32[]{:S(2)}) copy-start(s32[64]{0:T(128)} %param.13) | copy-start | bytes 772
  17.2 30.7 %all-to-all-start = ((bf16[64,32,128]{2,1,0:T(8,128)(2,1)}), bf16[64,32,128]{2,1,0:T(8,128)(2,1)S(1)}, u32[]{:S(2)}, u32[]{:S(2)}) async-start(bf16[64,32,128]{2,1,0:T(8,128)(2,1)} %broadcast_select_fusion), calls=%async_computation | async-start | bytes 1048576 | tf_op jit(solution)/shard_map/all_to_all | solution.py:20
  30.2 0.6 copy-start.9
  42.4 0.5 copy-start.5
  43.0 4.9 %copy-start.7 = (s32[64]{0:T(128)}, s32[64]{0:T(128)S(1)}, u32[]{:S(2)}) copy-start(s32[64]{0:T(128)S(1)} %compare_select_fusion.4) | copy-start | bytes 772
  56.1 5.7 %copy-start.8 = (s32[64]{0:T(128)S(1)}, s32[64]{0:T(128)}, u32[]{:S(2)}) copy-start(s32[64]{0:T(128)} %copy-done.7) | copy-start | bytes 772
  61.8 8.8 %copy-start.4 = (bf16[128,256]{1,0:T(8,128)(2,1)S(1)}, bf16[128,256]{1,0:T(8,128)(2,1)}, u32[]{:S(2)}) copy-start(bf16[128,256]{1,0:T(8,128)(2,1)} %param.10) | copy-start | bytes 196612
  61.8 8.8 %copy-start.10 = (bf16[512,256]{1,0:T(8,128)(2,1)S(1)}, bf16[512,256]{1,0:T(8,128)(2,1)}, u32[]{:S(2)}) copy-start(bf16[512,256]{1,0:T(8,128)(2,1)} %param.11) | copy-start | bytes 786436
  90.2 2.1 copy-start.6
  113.6 1.1 copy-start.2
  114.7 9.4 %copy-start.3 = (s32[64,32]{0,1:T(8,128)S(1)}, s32[64,32]{0,1:T(8,128)}, u32[]{:S(2)}) copy-start(s32[64,32]{0,1:T(8,128)} %param.16) | copy-start | bytes 24580
  115.8 36.3 %all-to-all-start.1 = ((bf16[64,32,256]{2,1,0:T(8,128)(2,1)}), bf16[64,32,256]{2,1,0:T(8,128)(2,1)}, u32[]{:S(2)}, u32[]{:S(2)}) async-start(bf16[64,32,256]{2,1,0:T(8,128)(2,1)} %bitcast.9), calls=%async_computation.1 | async-start | bytes 2097152 | tf_op jit(solution)/shard_map/all_to_all | solution.py:53
  124.1 43.2 %reduce-scatter.2.cloned.1.call-start = ((), (), s32[]{:S(2)}) async-start(), calls=%async_computation.4 | async-start | bytes 327680 | tf_op jit(solution)/shard_map/reduce_scatter | solution.py:63
  126.0 247.6 %all-reduce.2.cloned.1.call-start = ((), (), s32[]{:S(2)}) async-start(), calls=%async_computation.3 | async-start | bytes 262144 | tf_op jit(solution)/shard_map/psum | solution.py:66
Sparse Core Ops, SparseCore 0:
  128.0 22.4 reduce-scatter.1
Sparse Core Ops, SparseCore 1:
  132.6 241.0 all-reduce.1
where the time goes:
time: 384 us; the launch traced here: 383 us
  waiting for transfers between devices  232 us (60%)
  other arithmetic  50.9 us (13%)
  local copies, waits for them, and re-layouts  36.5 us (10%)
  starting transfers between devices  21.4 us (6%)
  between operations  15.7 us (4%)
  matrix products  14.9 us (4%)
  blocking collectives  10.9 us (3%)
    psum x1, waiting for transfers between devices, body(): weight_grad = lax.psum(weight_part, ('blk', 'grp'))  203 us
    all_to_all x1, waiting for transfers between devices, body(): lax.all_to_all(source_grad[row_count:boundary_end].reshape(block_count, s...  24 us
    scatter-add x1, other arithmetic, body(): jnp.zeros((source_tiles, tile_size, width_out), jnp.float32).at[tile_col]  19.2 us
    all_to_all x1, starting transfers between devices, body(): lax.all_to_all(outgoing, 'blk', split_axis=0, concat_axis=0, tiled=True)  13 us
    scatter-add x1, other arithmetic, body(): source_grad[:row_count].at[send_index.reshape(-1)]  12.4 us
    all_gather x1, blocking collectives, body(): hub_table = lax.all_gather(features[hub_index], 'grp', axis=0, tiled=True)  10.9 us
    dot_general x1, local copies, waits for them, and re-layouts, body(): jnp.einsum('lij,lif->ljf', tiles, pre_grad.reshape(row_tiles, tile_size,...  9.02 us
    scatter-add x1, other arithmetic, body(): jnp.zeros((row_tiles, tile_size, width_in), jnp.float32).at[tile_row]  8.77 us
  transfers between devices with their start and end apart: 4, of which 3 were waited for; matrix products, arithmetic and copies ran while one was open for 6% of the time, Pallas kernels for 0%

commit v1 on v0

v1 whole, which is shorter than its diff:
```python
import functools

import jax
import jax.numpy as jnp
from jax import lax
from jax.experimental import pallas as pl
from jax.experimental.pallas import tpu as pltpu
from jax.sharding import PartitionSpec as P

TILE = 128
MESH = pl.DeviceIdType.MESH
BF16 = jnp.bfloat16
F32 = jnp.float32


def dot(left, right):
    return lax.dot_general(left, right, (((1,), (0,)), ((), ())), preferred_element_type=F32)


def dot_t(left, right):
    return lax.dot_general(left, right, (((0,), (0,)), ((), ())), preferred_element_type=F32)


def iota(shape, axis):
    return lax.broadcasted_iota(jnp.int32, shape, axis)


def kernel(
    nb, ng, inner,
    feat_h, w_h, wt_h, cot_h, tiles_h, trow_h, tcol_h, hub_h, sidx_h, scnt_h,
    act_h, wg_h, fg_h,
    feat, w, wt, cot, tiles, trow, tcol, hub, sidx, scnt,
    cntm, idxm, sendbuf, incoming, hubs, hubsend, ohT, ohhubT,
    info, info_s, run, runT, A, AT, agg, aggb, pg, gb, act, retbuf, ret, hubret_send, hubret,
    part, ybuf, q3, xbuf, zbuf, zown, f3, wbuf, wg, own,
    in_sems, s1, r1, sh1, rh1, s2, r2, sh2, rh2, ar_s, ar_r, loc_sem, out_sems,
):
    rows = feat.shape[0]
    row_tiles = rows // TILE
    slots = sidx.shape[1]
    per_chunk = TILE // slots
    chunks = nb // per_chunk
    tile_count = tiles.shape[0]
    nz = nb // inner
    halves = inner // per_chunk
    src_tiles = row_tiles + chunks + ng
    b = lax.axis_index("blk")
    g = lax.axis_index("grp")
    z = b // inner
    ii = lax.rem(b, inner)
    half = ii // per_chunk
    lane_dev = lax.rem(b, per_chunk)

    ins = [
        (sidx_h, sidx.at[pl.ds(0, nb)]), (scnt_h, scnt), (feat_h, feat), (hub_h, hub), (trow_h, trow),
        (tcol_h, tcol), (tiles_h, tiles), (w_h, w), (wt_h, wt), (cot_h, cot),
    ]
    loads = [pltpu.make_async_copy(h, v, in_sems.at[i]) for i, (h, v) in enumerate(ins)]
    for load in loads:
        load.start()

    barrier = pltpu.get_barrier_semaphore()

    def greet_blk(k, _):
        pl.semaphore_signal(barrier, inc=1, device_id=(lax.rem(b + k, nb), g), device_id_type=MESH)
        return 0

    def greet_grp(k, _):
        pl.semaphore_signal(barrier, inc=1, device_id=(b, lax.rem(g + k, ng)), device_id_type=MESH)
        return 0

    lax.fori_loop(1, nb, greet_blk, 0)
    lax.fori_loop(1, ng, greet_grp, 0)

    loads[0].wait()
    loads[1].wait()
    lane1 = iota((1, TILE), 1)
    for i in range(chunks):
        row = jnp.full((1, TILE), scnt[i * per_chunk], jnp.int32)
        for q in range(1, per_chunk):
            row = jnp.where(lane1 >= q * slots, scnt[i * per_chunk + q], row)
        cntm[i:i + 1, :] = row
    idx = jnp.concatenate(
        [sidx[pl.ds(q, chunks, stride=per_chunk), :] for q in range(per_chunk)], axis=1
    )
    slot_of = lax.rem(iota((chunks, TILE), 1), slots)
    idxm[0:chunks, :] = jnp.where(slot_of < cntm[0:chunks, :], idx, -1).astype(F32)
    loads[3].wait()
    idxm[chunks:chunks + 1, :] = hub[...].astype(F32)
    loads[2].wait()

    pl.semaphore_wait(barrier, nb - 1 + ng - 1)

    lane_rows = iota((TILE, rows), 1).astype(F32)

    def gather(row):
        column = jnp.transpose(jnp.broadcast_to(row, (TILE, TILE)))
        wide = jnp.concatenate([column] * row_tiles, axis=1)
        onehot = jnp.where(wide == lane_rows, 1.0, 0.0).astype(BF16)
        return dot(onehot, feat[...]).astype(BF16)

    def chunk_at(j):
        m = j // halves
        e = lax.rem(j, halves)
        step = (m + 1) // 2
        dz = jnp.where(lax.rem(m, 2) == 1, nz // 2 - step, nz - nz // 2 + step)
        return lax.rem(z + dz, nz) * halves + lax.rem(half + e, halves)

    def exchange(buffer, landing, ssem, rsem, j, ci):
        for q in range(per_chunk):
            piece = lax.rem(lane_dev + q, per_chunk)
            source = buffer.at[j, pl.ds(pl.multiple_of(piece * slots, slots), slots)]
            target = landing.at[pl.ds(pl.multiple_of(b * slots, slots), slots)]
            to = ci * per_chunk + piece

            def send(source=source, target=target, to=to):
                pltpu.make_async_remote_copy(
                    src_ref=source, dst_ref=target, send_sem=ssem, recv_sem=rsem,
                    device_id=(to, g), device_id_type=MESH,
                ).start()

            if q == 0:
                @pl.when(to != b)
                def _():
                    send()

                @pl.when(to == b)
                def _():
                    pltpu.make_async_copy(source, target, rsem).start()
            else:
                send()

    hubsend[...] = gather(idxm[chunks:chunks + 1, :])
    hubs[g] = hubsend[...]
    for k in range(1, ng):
        pltpu.make_async_remote_copy(
            src_ref=hubsend, dst_ref=hubs.at[g], send_sem=sh1, recv_sem=rh1,
            device_id=(b, lax.rem(g + k, ng)), device_id_type=MESH,
        ).start()

    def send_chunk(j, _):
        ci = chunk_at(j)
        sendbuf[j] = gather(idxm[pl.ds(ci, 1), :])
        exchange(sendbuf, incoming, s1, r1, j, ci)
        return 0

    lax.fori_loop(0, chunks, send_chunk, 0)

    loads[4].wait()
    loads[5].wait()
    cells = row_tiles * src_tiles
    pad = jnp.full((1, TILE - tile_count), cells + 4, jnp.int32)
    key = jnp.concatenate([trow[...] * src_tiles + tcol[...], pad], axis=1) if tile_count < TILE else trow[...] * src_tiles + tcol[...]
    full = (TILE, TILE)
    lane = iota(full, 1)
    sub = iota(full, 0)

    def count(mask, values=1):
        return jnp.sum(jnp.where(mask, values, 0), axis=0, keepdims=True)

    key_l = jnp.broadcast_to(key, full)
    key_s = jnp.transpose(key_l)
    before = jnp.logical_or(key_s < key_l, jnp.logical_and(key_s == key_l, sub < lane))
    rank_s = jnp.transpose(jnp.broadcast_to(count(before), full))
    sorted_key = count(rank_s == lane, key_s)
    former_key = count(rank_s == lane - 1, key_s)
    first = jnp.where(jnp.logical_or(sorted_key != former_key, lane[0:1] == 0), 1, 0)
    upto = count(key_s <= lane)
    last = jnp.where(count(key_s == lane) > 0, upto - 1, tile_count)
    info[0:1, :] = jnp.clip(count(rank_s == lane, sub), 0, tile_count - 1)
    info[1:2, :] = first
    info[2:3, :] = jnp.clip(last, 0, tile_count)
    info[3:8, :] = jnp.zeros((5, TILE), jnp.int32)
    to_scalars = pltpu.make_async_copy(info, info_s, loc_sem)
    to_scalars.start()
    to_scalars.wait()

    loads[6].wait()
    run[tile_count] = jnp.zeros(full, BF16)
    runT[tile_count] = jnp.zeros(full, BF16)

    def add_tile(k, total):
        value = tiles[jnp.clip(info_s[0, k], 0, tile_count - 1)].astype(F32)
        total = jnp.where(info_s[1, k] == 1, value, total + value)
        run[k] = total.astype(BF16)
        runT[k] = jnp.transpose(total).astype(BF16)
        return total

    lax.fori_loop(0, tile_count, add_tile, jnp.zeros(full, F32))

    def place(c, _):
        at = pl.ds(pl.multiple_of(c * TILE, TILE), TILE)
        for r in range(row_tiles):
            cell = jnp.clip(info_s[2, r * src_tiles + c], 0, tile_count)
            A[r * TILE:(r + 1) * TILE, at] = run[cell]
            AT[c, :, r * TILE:(r + 1) * TILE] = runT[cell]
        return 0

    lax.fori_loop(0, src_tiles, place, 0)

    sub_rows = iota((rows, TILE), 0).astype(F32)

    def columns(i, _):
        row = idxm[pl.ds(i, 1), :]
        ohT[:, pl.ds(pl.multiple_of(i * TILE, TILE), TILE)] = jnp.where(sub_rows == row, 1.0, 0.0).astype(BF16)
        return 0

    lax.fori_loop(0, chunks, columns, 0)
    ohhubT[...] = jnp.where(sub_rows == idxm[chunks:chunks + 1, :], 1.0, 0.0).astype(BF16)

    lo, hi = rows, rows + chunks * TILE
    pltpu.make_async_copy(hubs.at[pl.ds(0, ng - 1)], hubs.at[pl.ds(0, ng - 1)], rh1).wait()
    agg[...] = dot(A[:, 0:lo], feat[...]) + dot(A[:, hi:], hubs[...].reshape(ng * TILE, TILE))
    for i in range(7, 10):
        loads[i].wait()
    pltpu.make_async_copy(incoming, incoming, r1).wait()
    for r in range(row_tiles):
        at = slice(r * TILE, (r + 1) * TILE)
        summed = (agg[at, :] + dot(A[at, lo:hi], incoming[...])).astype(BF16)
        aggb[at, :] = summed
        preact = dot(summed, w[...])
        logistic = 1.0 / (1.0 + jnp.exp(-preact))
        act[at, :] = (preact * logistic).astype(BF16)
        grad = (cot[at, :].astype(F32) * (logistic * (1.0 + preact * (1.0 - logistic)))).astype(BF16)
        pg[at, :] = grad
        gb[at, :] = dot(grad, wt[...]).astype(BF16)
    act_out = pltpu.make_async_copy(act, act_h, out_sems.at[0])
    act_out.start()

    part[...] = dot_t(aggb[...], pg[...])
    q_rows = TILE // ng

    def q_of(k):
        return part.at[pl.ds(pl.multiple_of(k * q_rows, q_rows), q_rows)]

    for k in range(1, ng):
        to = lax.rem(g + k, ng)
        pltpu.make_async_remote_copy(
            src_ref=q_of(to), dst_ref=ybuf.at[ng - 1 - k], send_sem=ar_s.at[0], recv_sem=ar_r.at[0],
            device_id=(b, to), device_id_type=MESH,
        ).start()

    def back_chunk(j, _):
        ci = chunk_at(j)
        retbuf[j] = dot(AT[row_tiles + ci], gb[...]).astype(BF16)
        exchange(retbuf, ret, s2, r2, j, ci)
        return 0

    lax.fori_loop(0, chunks, back_chunk, 0)
    for k in range(ng):
        hubret_send[k] = dot(AT[row_tiles + chunks + k], gb[...]).astype(BF16)
    for k in range(1, ng):
        to = lax.rem(g + k, ng)
        pltpu.make_async_remote_copy(
            src_ref=hubret_send.at[to], dst_ref=hubret.at[ng - 1 - k], send_sem=sh2, recv_sem=rh2,
            device_id=(b, to), device_id_type=MESH,
        ).start()
    for r in range(row_tiles):
        own[r * TILE:(r + 1) * TILE, :] = dot(AT[r], gb[...])

    pltpu.make_async_copy(ybuf, ybuf, ar_r.at[0]).wait()
    quarter = part[pl.ds(pl.multiple_of(g * q_rows, q_rows), q_rows), :]
    for k in range(ng - 1):
        quarter = quarter + ybuf[k]
    blocks = q3.shape[1]
    wide = w.shape[1] // TILE
    for n in range(inner * blocks):
        q3[n // blocks, n % blocks] = quarter[(n // wide) * 8:(n // wide) * 8 + 8, (n % wide) * TILE:(n % wide + 1) * TILE]

    def to_inner(k, _):
        to = lax.rem(ii + k, inner)
        pltpu.make_async_remote_copy(
            src_ref=q3.at[to], dst_ref=xbuf.at[inner - 1 - k], send_sem=ar_s.at[1], recv_sem=ar_r.at[1],
            device_id=(z * inner + to, g), device_id_type=MESH,
        ).start()
        return 0

    lax.fori_loop(1, inner, to_inner, 0)
    pltpu.make_async_copy(xbuf, xbuf, ar_r.at[1]).wait()
    eighth = q3[ii]
    for k in range(inner - 1):
        eighth = eighth + xbuf[k]
    zown[...] = eighth

    def to_z(k, _):
        pltpu.make_async_remote_copy(
            src_ref=zown, dst_ref=zbuf.at[z], send_sem=ar_s.at[2], recv_sem=ar_r.at[2],
            device_id=(lax.rem(z + k, nz) * inner + ii, g), device_id_type=MESH,
        ).start()
        return 0

    lax.fori_loop(1, nz, to_z, 0)
    zbuf[z] = eighth
    if nz > 1:
        pltpu.make_async_copy(zbuf.at[pl.ds(0, nz - 1)], zbuf.at[pl.ds(0, nz - 1)], ar_r.at[2]).wait()
    total = zbuf[0]
    for k in range(1, nz):
        total = total + zbuf[k]
    f3[ii] = total
    zown2 = f3.at[ii]

    def from_inner(k, _):
        pltpu.make_async_remote_copy(
            src_ref=zown2, dst_ref=f3.at[ii], send_sem=ar_s.at[3], recv_sem=ar_r.at[3],
            device_id=(z * inner + lax.rem(ii + k, inner), g), device_id_type=MESH,
        ).start()
        return 0

    lax.fori_loop(1, inner, from_inner, 0)
    pltpu.make_async_copy(f3.at[pl.ds(0, inner - 1)], f3.at[pl.ds(0, inner - 1)], ar_r.at[3]).wait()
    wbuf[g] = f3[...]
    for k in range(1, ng):
        pltpu.make_async_remote_copy(
            src_ref=f3, dst_ref=wbuf.at[g], send_sem=ar_s.at[4], recv_sem=ar_r.at[4],
            device_id=(b, lax.rem(g + k, ng)), device_id_type=MESH,
        ).start()
    pltpu.make_async_copy(wbuf.at[pl.ds(0, ng - 1)], wbuf.at[pl.ds(0, ng - 1)], ar_r.at[4]).wait()
    for k in range(ng):
        for n in range(inner * blocks):
            top = k * q_rows + (n // wide) * 8
            wg[top:top + 8, (n % wide) * TILE:(n % wide + 1) * TILE] = wbuf[k, n // blocks, n % blocks]
    wg_out = pltpu.make_async_copy(wg, wg_h, out_sems.at[1])
    wg_out.start()

    pltpu.make_async_copy(hubret, hubret, rh2).wait()
    hub_sum = hubret_send[g].astype(F32)
    for k in range(ng - 1):
        hub_sum = hub_sum + hubret[k].astype(F32)
    hub_hi = hub_sum.astype(BF16)
    hub_lo = (hub_sum - hub_hi.astype(F32)).astype(BF16)
    own[...] = own[...] + dot(ohhubT[...], hub_hi) + dot(ohhubT[...], hub_lo)
    pltpu.make_async_copy(ret, ret, r2).wait()
    for r in range(row_tiles):
        at = slice(r * TILE, (r + 1) * TILE)
        own[at, :] = own[at, :] + dot(ohT[at, :], ret[...])
    fg_out = pltpu.make_async_copy(own, fg_h, out_sems.at[2])
    fg_out.start()

    flat = pl.ds(0, (nb - 1) * slots)
    drop = ret.at[flat]
    pltpu.make_async_copy(drop, drop, s1).wait()
    pltpu.make_async_copy(drop, drop, s2).wait()
    pltpu.make_async_copy(hubret, hubret, sh1).wait()
    pltpu.make_async_copy(hubret, hubret, sh2).wait()
    pltpu.make_async_copy(ybuf, ybuf, ar_s.at[0]).wait()
    pltpu.make_async_copy(xbuf, xbuf, ar_s.at[1]).wait()
    if nz > 1:
        pltpu.make_async_copy(zbuf.at[pl.ds(0, nz - 1)], zbuf.at[pl.ds(0, nz - 1)], ar_s.at[2]).wait()
    pltpu.make_async_copy(xbuf, xbuf, ar_s.at[3]).wait()
    pltpu.make_async_copy(wbuf.at[pl.ds(0, ng - 1)], wbuf.at[pl.ds(0, ng - 1)], ar_s.at[4]).wait()
    act_out.wait()
    wg_out.wait()
    fg_out.wait()


def body(nb, ng, features, weight, cotangent, tiles, tile_row, tile_col, hub_index, send_index, send_count):
    rows, fin = features.shape
    fout = weight.shape[1]
    tile_count = tiles.shape[0]
    slots = send_index.shape[1]
    inner = 8
    nz = nb // inner
    chunks = nb * slots // TILE
    row_tiles = rows // TILE
    src_tiles = row_tiles + chunks + ng
    idx_rows = (chunks + 8) // 8 * 8
    blocks = (TILE // ng // 8) * (fout // TILE) // inner
    vm = pltpu.VMEM
    dma = pltpu.SemaphoreType.DMA
    scratch = [
        vm((rows, fin), BF16), vm((fin, fout), BF16), vm((fout, fin), BF16), vm((rows, fout), BF16),
        vm((tile_count, TILE, TILE), BF16), vm((1, tile_count), jnp.int32), vm((1, tile_count), jnp.int32),
        vm((1, TILE), jnp.int32), vm((nb + 8, slots), jnp.int32), pltpu.SMEM((nb,), jnp.int32),
        vm((idx_rows, TILE), jnp.int32), vm((idx_rows, TILE), F32), vm((chunks, TILE, fin), BF16),
        vm((nb * slots, fin), BF16), vm((ng, TILE, fin), BF16), vm((TILE, fin), BF16),
        vm((rows, chunks * TILE), BF16), vm((rows, TILE), BF16),
        vm((8, TILE), jnp.int32), pltpu.SMEM((8, TILE), jnp.int32),
        vm((tile_count + 1, TILE, TILE), BF16), vm((tile_count + 1, TILE, TILE), BF16),
        vm((rows, src_tiles * TILE), BF16), vm((src_tiles, TILE, rows), BF16),
        vm((rows, fin), F32), vm((rows, fin), BF16), vm((rows, fout), BF16), vm((rows, fin), BF16),
        vm((rows, fout), BF16), vm((chunks, TILE, fin), BF16), vm((nb * slots, fin), BF16),
        vm((ng, TILE, fin), BF16), vm((ng - 1, TILE, fin), BF16),
        vm((fin, fout), F32), vm((ng - 1, TILE // ng, fout), F32), vm((inner, blocks, 8, TILE), F32),
        vm((inner - 1, blocks, 8, TILE), F32), vm((nz, blocks, 8, TILE), F32), vm((blocks, 8, TILE), F32),
        vm((inner, blocks, 8, TILE), F32), vm((ng, inner, blocks, 8, TILE), F32), vm((fin, fout), F32),
        vm((rows, fin), F32),
        dma((10,)), dma, dma, dma, dma, dma, dma, dma, dma, dma((5,)), dma((5,)), dma, dma((3,)),
    ]
    flops = 2 * (2 * rows * src_tiles * TILE * fin + 2 * rows * chunks * TILE * fin + 3 * rows * fin * fout)
    return pl.pallas_call(
        functools.partial(kernel, nb, ng, inner),
        out_shape=[
            jax.ShapeDtypeStruct((rows, fout), BF16),
            jax.ShapeDtypeStruct((fin, fout), F32),
            jax.ShapeDtypeStruct((rows, fin), F32),
        ],
        in_specs=[pl.BlockSpec(memory_space=pl.ANY)] * 10,
        out_specs=[pl.BlockSpec(memory_space=pl.ANY)] * 3,
        scratch_shapes=scratch,
        compiler_params=pltpu.CompilerParams(
            collective_id=0, has_side_effects=True, vmem_limit_bytes=48 * 1024 * 1024
        ),
        cost_estimate=pl.CostEstimate(flops=flops, bytes_accessed=4 * 1024 * 1024, transcendentals=rows * fout),
    )(
        features, weight, weight.T, cotangent, tiles, tile_row.reshape(1, tile_count),
        tile_col.reshape(1, tile_count), hub_index.reshape(1, TILE), send_index, send_count,
    )


def solution(mesh):
    both = ("blk", "grp")
    return jax.shard_map(
        functools.partial(body, mesh.shape["blk"], mesh.shape["grp"]),
        mesh=mesh,
        in_specs=(
            P(both, None), P(), P(both, None), P(both, None, None), P(both), P(both), P(both),
            P(both, None), P(both),
        ),
        out_specs=(P(both, None), P(), P(both, None)),
        check_vma=False,
    )
```

time: 384 us -> 66.6 us (0.17)
  waiting for transfers between devices: 232 us -> 0 us
  Pallas kernels: 0 us -> 54.9 us
  other arithmetic: 50.9 us -> 0 us
  local copies, waits for them, and re-layouts: 36.5 us -> 10.7 us
  starting transfers between devices: 21.4 us -> 0 us
  between operations: 15.7 us -> 0.66 us
  matrix products: 14.9 us -> 0 us
  blocking collectives: 10.9 us -> 0 us
    psum x1 -> x0, waiting for transfers between devices: 203 us -> none  [body(): weight_grad = lax.psum(weight_part, ('blk', 'grp'))]
    pallas_call x0 -> x1, Pallas kernels: none -> 54.9 us  [body(): pl.pallas_call(functools.partial(kernel, nb, ng, inner), out_shape=[jax.S...]
    scatter-add x4 -> x0, other arithmetic: 42.1 us -> none  [the longest x1 19.2 us: body(): jnp.zeros((source_tiles, tile_size, width_out), jnp.float32).at[tile_col]]
    all_to_all x2 -> x0, waiting for transfers between devices: 28.9 us -> none  [the longest x1 24 us: body(): lax.all_to_all(source_grad[row_count:boundary_end].reshape(block_count, s...]
    all_to_all x2 -> x0, starting transfers between devices: 21.3 us -> none  [the longest x1 13 us: body(): lax.all_to_all(outgoing, 'blk', split_axis=0, concat_axis=0, tiled=True)]
    dot_general x5 -> x0, matrix products: 14.9 us -> none  [the longest x1 6.71 us: body(): jnp.einsum('lij,lif->ljf', tiles, pre_grad.reshape(row_tiles, tile_size,...]
    dot_general x2 -> x0, local copies, waits for them, and re-layouts: 14.7 us -> none  [the longest x1 9.02 us: body(): jnp.einsum('lij,lif->ljf', tiles, pre_grad.reshape(row_tiles, tile_size,...]
    gather x4 -> x0, local copies, waits for them, and re-layouts: 11.8 us -> none  [the longest x1 6.18 us: body(): features[send_index]]
  transfers between devices with their start and end apart: 4 -> 0, of which waited for: 3 -> 0; matrix products, arithmetic and copies ran while one was open for 6% -> 0% of each run, Pallas kernels for 0% -> 0%
where the time goes in v1:
time: 66.6 us; the launch traced here: 66.3 us
  Pallas kernels  54.9 us (82%)
  local copies, waits for them, and re-layouts  10.7 us (16%)
    pallas_call x1, Pallas kernels, body(): pl.pallas_call(functools.partial(kernel, nb, ng, inner), out_shape=[jax.S...  54.9 us
    unnamed x21, local copies, waits for them, and re-layouts  10.7 us

profile of v1, /device:TPU:1, one launch (start us, length us, event | category | flops | bytes accessed | tf_op | source)
XLA Modules:
  0.0 66.3 jit_solution(12764913810981203558)
XLA Ops:
  0.6 0.8 %copy.13.sidx_h = s32[64,32]{1,0:T(8,128)S(1)} copy(s32[64,32]{0,1:T(8,128)} %param.16) | data formatting | bytes 16384 | tf_op args[7]
  1.4 1.0 %copy.12 = bf16[128,256]{0,1:T(8,128)(2,1)S(1)} copy(bf16[128,256]{1,0:T(8,128)(2,1)} %w_h.1) | data formatting | bytes 131072 | tf_op args[1]
  2.4 0.0 copy-start
  2.4 0.8 %copy-done = bf16[128,256]{1,0:T(8,128)(2,1)S(1)} copy-done((bf16[128,256]{1,0:T(8,128)(2,1)S(1)}, bf16[128,256]{1,0:T(8,128)(2,1)}, u32[]{:S(2)}) %copy-start) | copy-done | bytes 65560
  3.2 0.0 copy-start.1
  3.2 1.6 %copy-done.1 = bf16[64,128,128]{2,1,0:T(8,128)(2,1)S(1)} copy-done((bf16[64,128,128]{2,1,0:T(8,128)(2,1)S(1)}, bf16[64,128,128]{2,1,0:T(8,128)(2,1)}, u32[]{:S(2)}) %copy-start.1) | copy-done | bytes 2097176
  4.8 0.0 copy-start.2
  4.8 0.9 %copy-done.2 = bf16[512,256]{1,0:T(8,128)(2,1)S(1)} copy-done((bf16[512,256]{1,0:T(8,128)(2,1)S(1)}, bf16[512,256]{1,0:T(8,128)(2,1)}, u32[]{:S(2)}) %copy-start.2) | copy-done | bytes 262168
  5.8 0.0 copy-start.3
  5.8 0.9 %copy-done.3 = bf16[512,128]{1,0:T(8,128)(2,1)S(1)} copy-done((bf16[512,128]{1,0:T(8,128)(2,1)S(1)}, bf16[512,128]{1,0:T(8,128)(2,1)}, u32[]{:S(2)}) %copy-start.3) | copy-done | bytes 131096
  6.7 0.0 copy-start.4
  6.7 0.7 copy-done.4
  7.3 0.0 copy-start.5
  7.3 0.7 copy-done.5
  8.0 0.0 copy-start.6
  8.0 0.7 copy-done.6
  8.6 0.0 copy-start.7
  8.6 0.7 copy-done.7
  9.3 54.9 %shard_map.112 = (bf16[512,256]{1,0:T(8,128)(2,1)S(1)}, f32[128,256]{1,0:T(8,128)S(1)}, f32[512,128]{1,0:T(8,128)S(1)}) custom-call(bf16[512,128]{1,0:T(8,128)(2,1)S(1)} %copy-done.3, bf16[128,256]{1,0:T(8,128)(2,1)S(1)} %copy-done, bf16[256,128]{1,0:T(8,128)(2,1)S(1)} %bitcast.4, bf16[512,256]{1,0:T(8,128)(2,1)S(1)} %copy-done.2, ...), custom_call_target="tpu_custom_call" | custom-call | flops 1442840576 | bytes 4194304 | tf_op jit(solution)/shard_map/pallas_call | solution.py:390
  64.2 0.7 %copy.17 = bf16[512,256]{1,0:T(8,128)(2,1)} copy(bf16[512,256]{1,0:T(8,128)(2,1)S(1)} %get-tuple-element.6) | data formatting | bytes 524288
  64.9 0.7 copy.18
  65.6 0.7 %copy.19 = f32[512,128]{1,0:T(8,128)} copy(f32[512,128]{1,0:T(8,128)S(1)} %get-tuple-element.8) | data formatting | bytes 524288
Async XLA Ops:
  2.4 0.8 %copy-start = (bf16[128,256]{1,0:T(8,128)(2,1)S(1)}, bf16[128,256]{1,0:T(8,128)(2,1)}, u32[]{:S(2)}) copy-start(bf16[128,256]{1,0:T(8,128)(2,1)} %w_h.1) | copy-start | bytes 196612
  3.2 1.6 %copy-start.1 = (bf16[64,128,128]{2,1,0:T(8,128)(2,1)S(1)}, bf16[64,128,128]{2,1,0:T(8,128)(2,1)}, u32[]{:S(2)}) copy-start(bf16[64,128,128]{2,1,0:T(8,128)(2,1)} %tiles_h.1) | copy-start | bytes 6291460
  4.8 0.9 %copy-start.2 = (bf16[512,256]{1,0:T(8,128)(2,1)S(1)}, bf16[512,256]{1,0:T(8,128)(2,1)}, u32[]{:S(2)}) copy-start(bf16[512,256]{1,0:T(8,128)(2,1)} %cot_h.1) | copy-start | bytes 786436
  5.8 0.9 %copy-start.3 = (bf16[512,128]{1,0:T(8,128)(2,1)S(1)}, bf16[512,128]{1,0:T(8,128)(2,1)}, u32[]{:S(2)}) copy-start(bf16[512,128]{1,0:T(8,128)(2,1)} %feat_h.1) | copy-start | bytes 393220
  6.7 0.7 copy-start.4
  7.3 0.7 copy-start.5
  8.0 0.7 copy-start.6
  8.6 0.7 copy-start.7

commit v2 on v1

v2 whole, which is shorter than its diff:
```python
import functools

import jax
import jax.numpy as jnp
from jax import lax
from jax.experimental import pallas as pl
from jax.experimental.pallas import tpu as pltpu
from jax.sharding import PartitionSpec as P

TILE = 128
MESH = pl.DeviceIdType.MESH
BF16 = jnp.bfloat16
F32 = jnp.float32


def dot(left, right):
    return lax.dot_general(left, right, (((1,), (0,)), ((), ())), preferred_element_type=F32)


def dot_t(left, right):
    return lax.dot_general(left, right, (((0,), (0,)), ((), ())), preferred_element_type=F32)


def iota(shape, axis):
    return lax.broadcasted_iota(jnp.int32, shape, axis)


def kernel(
    nb, ng, inner,
    feat_h, w_h, cot_h, tiles_h, trow_h, tcol_h, hub_h, sidx_h, scnt_h,
    act, wg, fg,
    feat, w, wt, cot, tiles, trow, tcol, hub, sidx_t, scnt, sidx,
    cntm, idxm, sendbuf, incoming, hubs, hubsend, ohT, ohhubT,
    info, info_s, run, runT, A, AT, agg, aggb, pg, gb, retbuf, ret, hubret_send, hubret,
    part, ybuf, q3, xbuf, zbuf, zown, f3, wbuf,
    in_sems, s1, r1, sh1, rh1, s2, r2, sh2, rh2, ar_s, ar_r, loc_sem,
):
    rows = feat.shape[0]
    row_tiles = rows // TILE
    slots = sidx_t.shape[0]
    per_chunk = TILE // slots
    chunks = nb // per_chunk
    tile_count = tiles.shape[0]
    nz = nb // inner
    halves = inner // per_chunk
    src_tiles = row_tiles + chunks + ng
    span = nz * TILE
    b = lax.axis_index("blk")
    g = lax.axis_index("grp")
    z = b // inner
    ii = lax.rem(b, inner)
    half = ii // per_chunk
    lane_dev = lax.rem(b, per_chunk)

    ins = [
        (sidx_h, sidx_t), (scnt_h, scnt), (feat_h, feat), (hub_h, hub), (trow_h, trow),
        (tcol_h, tcol), (tiles_h, tiles), (w_h, w), (cot_h, cot),
    ]
    loads = [pltpu.make_async_copy(h, v, in_sems.at[i]) for i, (h, v) in enumerate(ins)]
    for load in loads:
        load.start()

    barrier = pltpu.get_barrier_semaphore()

    def greet_blk(k, _):
        pl.semaphore_signal(barrier, inc=1, device_id=(lax.rem(b + k, nb), g), device_id_type=MESH)
        return 0

    def greet_grp(k, _):
        pl.semaphore_signal(barrier, inc=1, device_id=(b, lax.rem(g + k, ng)), device_id_type=MESH)
        return 0

    lax.fori_loop(1, nb, greet_blk, 0)
    lax.fori_loop(1, ng, greet_grp, 0)

    loads[0].wait()
    loads[1].wait()
    lane1 = iota((1, TILE), 1)
    for i in range(chunks):
        row = jnp.full((1, TILE), scnt[i * per_chunk], jnp.int32)
        for q in range(1, per_chunk):
            row = jnp.where(lane1 >= q * slots, scnt[i * per_chunk + q], row)
        cntm[i:i + 1, :] = row
    sidx[0:nb, :] = jnp.transpose(sidx_t[...])
    idx = jnp.concatenate(
        [sidx[pl.ds(q, chunks, stride=per_chunk), :] for q in range(per_chunk)], axis=1
    )
    slot_of = lax.rem(iota((chunks, TILE), 1), slots)
    idxm[0:chunks, :] = jnp.where(slot_of < cntm[0:chunks, :], idx, -1).astype(F32)
    loads[3].wait()
    idxm[chunks:chunks + 1, :] = hub[...].astype(F32)
    loads[2].wait()

    lane_rows = iota((TILE, rows), 1).astype(F32)

    def gather(row):
        column = jnp.transpose(jnp.broadcast_to(row, (TILE, TILE)))
        wide = jnp.concatenate([column] * row_tiles, axis=1)
        onehot = jnp.where(wide == lane_rows, 1.0, 0.0).astype(BF16)
        return dot(onehot, feat[...]).astype(BF16)

    rounds = [(e, q) for e in reversed(range(halves)) for q in reversed(range(per_chunk))]

    def to_z(m):
        step = (m + 1) // 2
        return lax.rem(z + jnp.where(lax.rem(m, 2) == 1, nz // 2 - step, nz - nz // 2 + step), nz)

    def to_half(e):
        return lax.rem(half + e, halves)

    mine = pl.ds(pl.multiple_of(((half * nz + z) * per_chunk + lane_dev) * slots, slots), slots)

    def exchange(buffer, landing, ssem, rsem, e, q):
        piece = lax.rem(lane_dev + q, per_chunk)

        def source(m):
            return buffer.at[e, m, pl.ds(pl.multiple_of(piece * slots, slots), slots)]

        def send(m, _):
            pltpu.make_async_remote_copy(
                src_ref=source(m), dst_ref=landing.at[mine], send_sem=ssem, recv_sem=rsem.at[e],
                device_id=((to_z(m) * halves + to_half(e)) * per_chunk + piece, g), device_id_type=MESH,
            ).start()
            return 0

        if e == 0 and q == 0:
            lax.fori_loop(0, nz - 1, send, 0)
            pltpu.make_async_copy(source(nz - 1), landing.at[mine], rsem.at[0]).start()
        else:
            lax.fori_loop(0, nz, send, 0)

    def landed(landing, rsem, e):
        some = landing.at[pl.ds(0, span)]
        pltpu.make_async_copy(some, some, rsem.at[e]).wait()
        return pl.ds(pl.multiple_of(to_half(e) * span, TILE), span)

    def gather_some(e, lo, hi):
        def at(m, _):
            sendbuf[e, m] = gather(idxm[pl.ds(to_z(m) * halves + to_half(e), 1), :])
            return 0

        lax.fori_loop(lo, hi, at, 0)

    hubsend[...] = gather(idxm[chunks:chunks + 1, :])
    hubs[g] = hubsend[...]
    gather_some(halves - 1, 0, nz)
    pl.semaphore_wait(barrier, nb - 1 + ng - 1)
    for k in range(1, ng):
        pltpu.make_async_remote_copy(
            src_ref=hubsend, dst_ref=hubs.at[g], send_sem=sh1, recv_sem=rh1,
            device_id=(b, lax.rem(g + k, ng)), device_id_type=MESH,
        ).start()

    def turns(produce, buffer, landing, ssem, rsem, between):
        for i, (e, q) in enumerate(rounds):
            exchange(buffer, landing, ssem, rsem, e, q)
            turn = i % per_chunk
            if e > 0:
                produce(e - 1, turn * nz // per_chunk, (turn + 1) * nz // per_chunk)
            between(i)

    turns(gather_some, sendbuf, incoming, s1, r1, lambda i: None)

    loads[4].wait()
    loads[5].wait()
    cells = row_tiles * src_tiles
    pad = jnp.full((1, TILE - tile_count), cells + 4, jnp.int32)
    key = jnp.concatenate([trow[...] * src_tiles + tcol[...], pad], axis=1) if tile_count < TILE else trow[...] * src_tiles + tcol[...]
    full = (TILE, TILE)
    lane = iota(full, 1)
    sub = iota(full, 0)

    def count(mask, values=1):
        return jnp.sum(jnp.where(mask, values, 0), axis=0, keepdims=True)

    key_l = jnp.broadcast_to(key, full)
    key_s = jnp.transpose(key_l)
    before = jnp.logical_or(key_s < key_l, jnp.logical_and(key_s == key_l, sub < lane))
    rank_s = jnp.transpose(jnp.broadcast_to(count(before), full))
    sorted_key = count(rank_s == lane, key_s)
    former_key = count(rank_s == lane - 1, key_s)
    first = jnp.where(jnp.logical_or(sorted_key != former_key, lane[0:1] == 0), 1, 0)
    upto = count(key_s <= lane)
    last = jnp.where(count(key_s == lane) > 0, upto - 1, tile_count)
    info[0:1, :] = jnp.clip(count(rank_s == lane, sub), 0, tile_count - 1)
    info[1:2, :] = first
    info[2:3, :] = jnp.clip(last, 0, tile_count)
    info[3:8, :] = jnp.zeros((5, TILE), jnp.int32)
    to_scalars = pltpu.make_async_copy(info, info_s, loc_sem)
    to_scalars.start()
    to_scalars.wait()

    loads[6].wait()
    run[tile_count] = jnp.zeros(full, BF16)
    runT[tile_count] = jnp.zeros(full, BF16)

    def add_tile(k, total):
        value = tiles[jnp.clip(info_s[0, k], 0, tile_count - 1)].astype(F32)
        total = jnp.where(info_s[1, k] == 1, value, total + value)
        run[k] = total.astype(BF16)
        runT[k] = jnp.transpose(total).astype(BF16)
        return total

    lax.fori_loop(0, tile_count, add_tile, jnp.zeros(full, F32))

    def place(c, _):
        bound = c - row_tiles
        moved = row_tiles + lax.rem(bound, halves) * nz + bound // halves
        within = jnp.logical_and(bound >= 0, bound < chunks)
        at = pl.ds(pl.multiple_of(jnp.where(within, moved, c) * TILE, TILE), TILE)
        for r in range(row_tiles):
            cell = jnp.clip(info_s[2, r * src_tiles + c], 0, tile_count)
            A[r * TILE:(r + 1) * TILE, at] = run[cell]
            AT[c, :, r * TILE:(r + 1) * TILE] = runT[cell]
        return 0

    lax.fori_loop(0, src_tiles, place, 0)

    sub_rows = iota((rows, TILE), 0).astype(F32)

    def columns(i, _):
        row = idxm[pl.ds(i, 1), :]
        place_at = lax.rem(i, halves) * nz + i // halves
        ohT[:, pl.ds(pl.multiple_of(place_at * TILE, TILE), TILE)] = jnp.where(sub_rows == row, 1.0, 0.0).astype(BF16)
        return 0

    lax.fori_loop(0, chunks, columns, 0)
    ohhubT[...] = jnp.where(sub_rows == idxm[chunks:chunks + 1, :], 1.0, 0.0).astype(BF16)

    lo, hi = rows, rows + chunks * TILE
    pltpu.make_async_copy(hubs.at[pl.ds(0, ng - 1)], hubs.at[pl.ds(0, ng - 1)], rh1).wait()
    agg[...] = dot(A[:, 0:lo], feat[...]) + dot(A[:, hi:], hubs[...].reshape(ng * TILE, TILE))
    for i in range(7, 9):
        loads[i].wait()
    wt[...] = jnp.transpose(w[...].astype(F32)).astype(BF16)

    for e in reversed(range(halves)):
        at = landed(incoming, r1, e)
        columns_at = pl.ds(pl.multiple_of(lo + to_half(e) * span, TILE), span)
        agg[...] = agg[...] + dot(A[:, columns_at], incoming[at, :])
    for r in range(row_tiles):
        at = slice(r * TILE, (r + 1) * TILE)
        summed = agg[at, :].astype(BF16)
        aggb[at, :] = summed
        preact = dot(summed, w[...])
        logistic = 1.0 / (1.0 + jnp.exp(-preact))
        act[at, :] = (preact * logistic).astype(BF16)
        grad = (cot[at, :].astype(F32) * (logistic * (1.0 + preact * (1.0 - logistic)))).astype(BF16)
        pg[at, :] = grad
        gb[at, :] = dot(grad, wt[...]).astype(BF16)

    part[...] = dot_t(aggb[...], pg[...])
    q_rows = TILE // ng

    def q_of(k):
        return part.at[pl.ds(pl.multiple_of(k * q_rows, q_rows), q_rows)]

    for k in range(1, ng):
        to = lax.rem(g + k, ng)
        pltpu.make_async_remote_copy(
            src_ref=q_of(to), dst_ref=ybuf.at[ng - 1 - k], send_sem=ar_s.at[0], recv_sem=ar_r.at[0],
            device_id=(b, to), device_id_type=MESH,
        ).start()

    blocks = q3.shape[1]
    wide = w.shape[1] // TILE
    most = pl.ds(0, inner - 1)

    def over_inner():
        pltpu.make_async_copy(ybuf, ybuf, ar_r.at[0]).wait()
        quarter = part[pl.ds(pl.multiple_of(g * q_rows, q_rows), q_rows), :]
        for k in range(ng - 1):
            quarter = quarter + ybuf[k]
        for n in range(inner * blocks):
            q3[n // blocks, n % blocks] = quarter[
                (n // wide) * 8:(n // wide) * 8 + 8, (n % wide) * TILE:(n % wide + 1) * TILE
            ]

        def to_inner(k, _):
            to = lax.rem(ii + k, inner)
            pltpu.make_async_remote_copy(
                src_ref=q3.at[to], dst_ref=xbuf.at[inner - 1 - k], send_sem=ar_s.at[1], recv_sem=ar_r.at[1],
                device_id=(z * inner + to, g), device_id_type=MESH,
            ).start()
            return 0

        lax.fori_loop(1, inner, to_inner, 0)

    def over_z():
        pltpu.make_async_copy(xbuf, xbuf, ar_r.at[1]).wait()
        eighth = q3[ii]
        for k in range(inner - 1):
            eighth = eighth + xbuf[k]
        zown[...] = eighth
        zbuf[z] = eighth

        def send_z(k, _):
            pltpu.make_async_remote_copy(
                src_ref=zown, dst_ref=zbuf.at[z], send_sem=ar_s.at[2], recv_sem=ar_r.at[2],
                device_id=(lax.rem(z + k, nz) * inner + ii, g), device_id_type=MESH,
            ).start()
            return 0

        lax.fori_loop(1, nz, send_z, 0)

    def back_inner():
        others = zbuf.at[pl.ds(0, nz - 1)]
        pltpu.make_async_copy(others, others, ar_r.at[2]).wait()
        total = zbuf[0]
        for k in range(1, nz):
            total = total + zbuf[k]
        f3[ii] = total

        def from_inner(k, _):
            pltpu.make_async_remote_copy(
                src_ref=f3.at[ii], dst_ref=f3.at[ii], send_sem=ar_s.at[3], recv_sem=ar_r.at[3],
                device_id=(z * inner + lax.rem(ii + k, inner), g), device_id_type=MESH,
            ).start()
            return 0

        lax.fori_loop(1, inner, from_inner, 0)

    def back_grp():
        pltpu.make_async_copy(f3.at[most], f3.at[most], ar_r.at[3]).wait()
        wbuf[g] = f3[...]
        for k in range(1, ng):
            pltpu.make_async_remote_copy(
                src_ref=f3, dst_ref=wbuf.at[g], send_sem=ar_s.at[4], recv_sem=ar_r.at[4],
                device_id=(b, lax.rem(g + k, ng)), device_id_type=MESH,
            ).start()

    def finish_weight():
        others = wbuf.at[pl.ds(0, ng - 1)]
        pltpu.make_async_copy(others, others, ar_r.at[4]).wait()
        for k in range(ng):
            for n in range(inner * blocks):
                top = k * q_rows + (n // wide) * 8
                wg[top:top + 8, (n % wide) * TILE:(n % wide + 1) * TILE] = wbuf[k, n // blocks, n % blocks]

    def back_some(e, lo, hi):
        def at(m, _):
            retbuf[e, m] = dot(AT[row_tiles + to_z(m) * halves + to_half(e)], gb[...]).astype(BF16)
            return 0

        lax.fori_loop(lo, hi, at, 0)

    def back_hubs():
        for k in range(ng):
            hubret_send[k] = dot(AT[row_tiles + chunks + k], gb[...]).astype(BF16)
        for k in range(1, ng):
            to = lax.rem(g + k, ng)
            pltpu.make_async_remote_copy(
                src_ref=hubret_send.at[to], dst_ref=hubret.at[ng - 1 - k], send_sem=sh2, recv_sem=rh2,
                device_id=(b, to), device_id_type=MESH,
            ).start()

    plan = {1: over_z, 2: back_hubs, 3: back_inner, 5: back_grp}
    back_some(halves - 1, 0, nz)
    over_inner()
    turns(back_some, retbuf, ret, s2, r2, lambda i: plan.get(i, lambda: None)())
    for r in range(row_tiles):
        fg[r * TILE:(r + 1) * TILE, :] = dot(AT[r], gb[...])
    finish_weight()

    pltpu.make_async_copy(hubret, hubret, rh2).wait()
    hub_sum = hubret_send[g].astype(F32)
    for k in range(ng - 1):
        hub_sum = hub_sum + hubret[k].astype(F32)
    hub_hi = hub_sum.astype(BF16)
    hub_lo = (hub_sum - hub_hi.astype(F32)).astype(BF16)
    fg[...] = fg[...] + dot(ohhubT[...], hub_hi) + dot(ohhubT[...], hub_lo)
    for e in reversed(range(halves)):
        at = landed(ret, r2, e)
        fg[...] = fg[...] + dot(ohT[:, at], ret[at, :])

    flat = pl.ds(0, (nb - 1) * slots)
    drop = ret.at[flat]
    pltpu.make_async_copy(drop, drop, s1).wait()
    pltpu.make_async_copy(drop, drop, s2).wait()
    pltpu.make_async_copy(hubret, hubret, sh1).wait()
    pltpu.make_async_copy(hubret, hubret, sh2).wait()
    pltpu.make_async_copy(ybuf, ybuf, ar_s.at[0]).wait()
    pltpu.make_async_copy(xbuf, xbuf, ar_s.at[1]).wait()
    pltpu.make_async_copy(zbuf.at[pl.ds(0, nz - 1)], zbuf.at[pl.ds(0, nz - 1)], ar_s.at[2]).wait()
    pltpu.make_async_copy(xbuf, xbuf, ar_s.at[3]).wait()
    pltpu.make_async_copy(wbuf.at[pl.ds(0, ng - 1)], wbuf.at[pl.ds(0, ng - 1)], ar_s.at[4]).wait()


def hand_out(a, b, c, a_out, b_out, c_out, sems):
    copies = [
        pltpu.make_async_copy(source, target, sems.at[i])
        for i, (source, target) in enumerate([(a, a_out), (b, b_out), (c, c_out)])
    ]
    for copy in copies:
        copy.start()
    for copy in copies:
        copy.wait()


def body(nb, ng, features, weight, cotangent, tiles, tile_row, tile_col, hub_index, send_index, send_count):
    rows, fin = features.shape
    fout = weight.shape[1]
    tile_count = tiles.shape[0]
    slots = send_index.shape[1]
    inner = 8
    nz = nb // inner
    chunks = nb * slots // TILE
    row_tiles = rows // TILE
    src_tiles = row_tiles + chunks + ng
    idx_rows = (chunks + 8) // 8 * 8
    blocks = (TILE // ng // 8) * (fout // TILE) // inner
    vm = pltpu.VMEM
    dma = pltpu.SemaphoreType.DMA
    scratch = [
        vm((rows, fin), BF16), vm((fin, fout), BF16), vm((fout, fin), BF16), vm((rows, fout), BF16),
        vm((tile_count, TILE, TILE), BF16), vm((1, tile_count), jnp.int32), vm((1, tile_count), jnp.int32),
        vm((1, TILE), jnp.int32), vm((slots, nb), jnp.int32), pltpu.SMEM((nb,), jnp.int32),
        vm((nb + 8, slots), jnp.int32),
        vm((idx_rows, TILE), jnp.int32), vm((idx_rows, TILE), F32), vm((2, nz, TILE, fin), BF16),
        vm((nb * slots, fin), BF16), vm((ng, TILE, fin), BF16), vm((TILE, fin), BF16),
        vm((rows, chunks * TILE), BF16), vm((rows, TILE), BF16),
        vm((8, TILE), jnp.int32), pltpu.SMEM((8, TILE), jnp.int32),
        vm((tile_count + 1, TILE, TILE), BF16), vm((tile_count + 1, TILE, TILE), BF16),
        vm((rows, src_tiles * TILE), BF16), vm((src_tiles, TILE, rows), BF16),
        vm((rows, fin), F32), vm((rows, fin), BF16), vm((rows, fout), BF16), vm((rows, fin), BF16),
        vm((2, nz, TILE, fin), BF16), vm((nb * slots, fin), BF16),
        vm((ng, TILE, fin), BF16), vm((ng - 1, TILE, fin), BF16),
        vm((fin, fout), F32), vm((ng - 1, TILE // ng, fout), F32), vm((inner, blocks, 8, TILE), F32),
        vm((inner - 1, blocks, 8, TILE), F32), vm((nz, blocks, 8, TILE), F32), vm((blocks, 8, TILE), F32),
        vm((inner, blocks, 8, TILE), F32), vm((ng, inner, blocks, 8, TILE), F32),
        dma((9,)), dma, dma((2,)), dma, dma, dma, dma((2,)), dma, dma, dma((5,)), dma((5,)), dma,
    ]
    flops = 2 * (2 * rows * src_tiles * TILE * fin + 2 * rows * chunks * TILE * fin + 3 * rows * fin * fout)
    results = pl.pallas_call(
        functools.partial(kernel, nb, ng, inner),
        out_shape=[vm((rows, fout), BF16), vm((fin, fout), F32), vm((rows, fin), F32)],
        in_specs=[pl.BlockSpec(memory_space=pl.ANY)] * 9,
        out_specs=[pl.BlockSpec(memory_space=pltpu.VMEM)] * 3,
        scratch_shapes=scratch,
        compiler_params=pltpu.CompilerParams(
            collective_id=0, has_side_effects=True, vmem_limit_bytes=56 * 1024 * 1024
        ),
        cost_estimate=pl.CostEstimate(flops=flops, bytes_accessed=4 * 1024 * 1024, transcendentals=rows * fout),
    )(
        features, weight, cotangent, tiles, tile_row.reshape(1, tile_count),
        tile_col.reshape(1, tile_count), hub_index.reshape(1, TILE), send_index.T, send_count,
    )
    return pl.pallas_call(
        hand_out,
        out_shape=[jax.ShapeDtypeStruct(result.shape, result.dtype) for result in results],
        in_specs=[pl.BlockSpec(memory_space=pl.ANY)] * 3,
        out_specs=[pl.BlockSpec(memory_space=pl.ANY)] * 3,
        scratch_shapes=[dma((3,))],
        compiler_params=pltpu.CompilerParams(vmem_limit_bytes=1024 * 1024),
    )(*results)


def solution(mesh):
    both = ("blk", "grp")
    return jax.shard_map(
        functools.partial(body, mesh.shape["blk"], mesh.shape["grp"]),
        mesh=mesh,
        in_specs=(
            P(both, None), P(), P(both, None), P(both, None, None), P(both), P(both), P(both),
            P(both, None), P(both),
        ),
        out_specs=(P(both, None), P(), P(both, None)),
        check_vma=False,
    )
```

time: 66.6 us -> 53.4 us (0.80)
  local copies, waits for them, and re-layouts: 10.7 us -> 0 us
  Pallas kernels: 54.9 us -> 52.7 us
    unnamed x21 -> x0, local copies, waits for them, and re-layouts: 10.7 us -> none
    pallas_call x1 -> x2, Pallas kernels: 54.9 us -> 52.7 us  [the longest x1 51.8 us: body(): pl.pallas_call(functools.partial(kernel, nb, ng, inner), out_shape=[vm((r...]
where the time goes in v2:
time: 53.4 us; the launch traced here: 53.3 us
  Pallas kernels  52.7 us (99%)
  between operations  0.64 us (1%)
    pallas_call x1, Pallas kernels, body(): pl.pallas_call(functools.partial(kernel, nb, ng, inner), out_shape=[vm((r...  51.8 us

profile of v2, /device:TPU:1, one launch (start us, length us, event | category | flops | bytes accessed | tf_op | source)
XLA Modules:
  0.0 53.3 jit_solution(17124578197643316890)
XLA Ops:
  0.6 51.8 %shard_map.112 = (bf16[512,256]{1,0:T(8,128)(2,1)S(1)}, f32[128,256]{1,0:T(8,128)S(1)}, f32[512,128]{1,0:T(8,128)S(1)}) custom-call(bf16[512,128]{1,0:T(8,128)(2,1)} %feat_h.1, bf16[128,256]{1,0:T(8,128)(2,1)} %w_h.1, bf16[512,256]{1,0:T(8,128)(2,1)} %cot_h.1, bf16[64,128,128]{2,1,0:T(8,128)(2,1)} %tiles_h.1, s32[1,64]{1,0:T(1,128)} %bitcast.5, ...), custom_call_target="tpu_custom_call" | custom-call | flops 1442840576 | bytes 4194304 | tf_op jit(solution)/shard_map/pallas_call | solution.py:434
  52.5 0.9 %shard_map.113 = (bf16[512,256]{1,0:T(8,128)(2,1)}, f32[128,256]{1,0:T(8,128)}, f32[512,128]{1,0:T(8,128)}) custom-call(bf16[512,256]{1,0:T(8,128)(2,1)S(1)} %get-tuple-element.6.a, f32[128,256]{1,0:T(8,128)S(1)} %get-tuple-element.7.b, f32[512,128]{1,0:T(8,128)S(1)} %get-tuple-element.8.c), custom_call_target="tpu_custom_call" | custom-call | tf_op jit(solution)/shard_map/pallas_call | solution.py:448

commit v3 on v2

--- a/solution.py
+++ b/solution.py
@@ -32,7 +32,7 @@
     feat, w, wt, cot, tiles, trow, tcol, hub, sidx_t, scnt, sidx,
     cntm, idxm, sendbuf, incoming, hubs, hubsend, ohT, ohhubT,
     info, info_s, run, runT, A, AT, agg, aggb, pg, gb, retbuf, ret, hubret_send, hubret,
-    part, ybuf, q3, xbuf, zbuf, zown, f3, wbuf,
+    part, q3, xbuf, zbuf, zown, f3,
     in_sems, s1, r1, sh1, rh1, s2, r2, sh2, rh2, ar_s, ar_r, loc_sem,
 ):
     rows = feat.shape[0]
@@ -51,6 +51,7 @@
     ii = lax.rem(b, inner)
     half = ii // per_chunk
     lane_dev = lax.rem(b, per_chunk)
+    u = g * inner + ii
 
     ins = [
         (sidx_h, sidx_t), (scnt_h, scnt), (feat_h, feat), (hub_h, hub), (trow_h, trow),
@@ -62,16 +63,20 @@
 
     barrier = pltpu.get_barrier_semaphore()
 
-    def greet_blk(k, _):
-        pl.semaphore_signal(barrier, inc=1, device_id=(lax.rem(b + k, nb), g), device_id_type=MESH)
+    def greet_z(k, _):
+        to = lax.rem(z * inner + k, nb)
+        pl.semaphore_signal(barrier, inc=1, device_id=(to, g), device_id_type=MESH)
         return 0
 
     def greet_grp(k, _):
-        pl.semaphore_signal(barrier, inc=1, device_id=(b, lax.rem(g + k, ng)), device_id_type=MESH)
+        to = lax.rem(u + k, ng * inner)
+        pl.semaphore_signal(barrier, inc=1, device_id=(z * inner + lax.rem(to, inner), to // inner), device_id_type=MESH)
         return 0
 
-    lax.fori_loop(1, nb, greet_blk, 0)
-    lax.fori_loop(1, ng, greet_grp, 0)
+    others = nb - inner + ng * inner - 1
+
+    lax.fori_loop(inner, nb, greet_z, 0)
+    lax.fori_loop(1, ng * inner, greet_grp, 0)
 
     loads[0].wait()
     loads[1].wait()
@@ -144,7 +149,7 @@
     hubsend[...] = gather(idxm[chunks:chunks + 1, :])
     hubs[g] = hubsend[...]
     gather_some(halves - 1, 0, nz)
-    pl.semaphore_wait(barrier, nb - 1 + ng - 1)
+    pl.semaphore_wait(barrier, others)
     for k in range(1, ng):
         pltpu.make_async_remote_copy(
             src_ref=hubsend, dst_ref=hubs.at[g], send_sem=sh1, recv_sem=rh1,
@@ -250,92 +255,55 @@
         gb[at, :] = dot(grad, wt[...]).astype(BF16)
 
     part[...] = dot_t(aggb[...], pg[...])
-    q_rows = TILE // ng
-
-    def q_of(k):
-        return part.at[pl.ds(pl.multiple_of(k * q_rows, q_rows), q_rows)]
-
-    for k in range(1, ng):
-        to = lax.rem(g + k, ng)
-        pltpu.make_async_remote_copy(
-            src_ref=q_of(to), dst_ref=ybuf.at[ng - 1 - k], send_sem=ar_s.at[0], recv_sem=ar_r.at[0],
-            device_id=(b, to), device_id_type=MESH,
-        ).start()
-
-    blocks = q3.shape[1]
+    members, blocks = q3.shape[0], q3.shape[1]
     wide = w.shape[1] // TILE
-    most = pl.ds(0, inner - 1)
-
-    def over_inner():
-        pltpu.make_async_copy(ybuf, ybuf, ar_r.at[0]).wait()
-        quarter = part[pl.ds(pl.multiple_of(g * q_rows, q_rows), q_rows), :]
-        for k in range(ng - 1):
-            quarter = quarter + ybuf[k]
-        for n in range(inner * blocks):
-            q3[n // blocks, n % blocks] = quarter[
-                (n // wide) * 8:(n // wide) * 8 + 8, (n % wide) * TILE:(n % wide + 1) * TILE
-            ]
-
-        def to_inner(k, _):
-            to = lax.rem(ii + k, inner)
+    for n in range(members * blocks):
+        q3[n // blocks, n % blocks] = part[(n // wide) * 8:(n // wide) * 8 + 8, (n % wide) * TILE:(n % wide + 1) * TILE]
+
+    def over_plane(source, target, i):
+        def send(k, _):
+            to = lax.rem(u + k, members)
             pltpu.make_async_remote_copy(
-                src_ref=q3.at[to], dst_ref=xbuf.at[inner - 1 - k], send_sem=ar_s.at[1], recv_sem=ar_r.at[1],
-                device_id=(z * inner + to, g), device_id_type=MESH,
+                src_ref=source(to), dst_ref=target(k), send_sem=ar_s.at[i], recv_sem=ar_r.at[i],
+                device_id=(z * inner + lax.rem(to, inner), to // inner), device_id_type=MESH,
             ).start()
             return 0
 
-        lax.fori_loop(1, inner, to_inner, 0)
+        lax.fori_loop(1, members, send, 0)
+
+    over_plane(lambda to: q3.at[to], lambda k: xbuf.at[members - 1 - k], 0)
 
     def over_z():
-        pltpu.make_async_copy(xbuf, xbuf, ar_r.at[1]).wait()
-        eighth = q3[ii]
-        for k in range(inner - 1):
-            eighth = eighth + xbuf[k]
-        zown[...] = eighth
-        zbuf[z] = eighth
+        pltpu.make_async_copy(xbuf, xbuf, ar_r.at[0]).wait()
+        summed = q3[u]
+        for k in range(members - 1):
+            summed = summed + xbuf[k]
+        zown[...] = summed
+        zbuf[z] = summed
 
         def send_z(k, _):
             pltpu.make_async_remote_copy(
-                src_ref=zown, dst_ref=zbuf.at[z], send_sem=ar_s.at[2], recv_sem=ar_r.at[2],
+                src_ref=zown, dst_ref=zbuf.at[z], send_sem=ar_s.at[1], recv_sem=ar_r.at[1],
                 device_id=(lax.rem(z + k, nz) * inner + ii, g), device_id_type=MESH,
             ).start()
             return 0
 
         lax.fori_loop(1, nz, send_z, 0)
 
-    def back_inner():
+    def back_plane():
         others = zbuf.at[pl.ds(0, nz - 1)]
-        pltpu.make_async_copy(others, others, ar_r.at[2]).wait()
+        pltpu.make_async_copy(others, others, ar_r.at[1]).wait()
         total = zbuf[0]
         for k in range(1, nz):
             total = total + zbuf[k]
-        f3[ii] = total
-
-        def from_inner(k, _):
-            pltpu.make_async_remote_copy(
-                src_ref=f3.at[ii], dst_ref=f3.at[ii], send_sem=ar_s.at[3], recv_sem=ar_r.at[3],
-                device_id=(z * inner + lax.rem(ii + k, inner), g), device_id_type=MESH,
-            ).start()
-            return 0
-
-        lax.fori_loop(1, inner, from_inner, 0)
-
-    def back_grp():
-        pltpu.make_async_copy(f3.at[most], f3.at[most], ar_r.at[3]).wait()
-        wbuf[g] = f3[...]
-        for k in range(1, ng):
-            pltpu.make_async_remote_copy(
-                src_ref=f3, dst_ref=wbuf.at[g], send_sem=ar_s.at[4], recv_sem=ar_r.at[4],
-                device_id=(b, lax.rem(g + k, ng)), device_id_type=MESH,
-            ).start()
+        f3[u] = total
+        over_plane(lambda to: f3.at[u], lambda k: f3.at[u], 2)
 
     def finish_weight():
-        others = wbuf.at[pl.ds(0, ng - 1)]
-        pltpu.make_async_copy(others, others, ar_r.at[4]).wait()
-        for k in range(ng):
-            for n in range(inner * blocks):
-                top = k * q_rows + (n // wide) * 8
-                wg[top:top + 8, (n % wide) * TILE:(n % wide + 1) * TILE] = wbuf[k, n // blocks, n % blocks]
+        others = f3.at[pl.ds(0, members - 1)]
+        pltpu.make_async_copy(others, others, ar_r.at[2]).wait()
+        for n in range(members * blocks):
+            wg[(n // wide) * 8:(n // wide) * 8 + 8, (n % wide) * TILE:(n % wide + 1) * TILE] = f3[n // blocks, n % blocks]
 
     def back_some(e, lo, hi):
         def at(m, _):
@@ -354,13 +322,11 @@
                 device_id=(b, to), device_id_type=MESH,
             ).start()
 
-    plan = {1: over_z, 2: back_hubs, 3: back_inner, 5: back_grp}
+    plan = {0: back_hubs, 2: over_z, 5: back_plane}
     back_some(halves - 1, 0, nz)
-    over_inner()
     turns(back_some, retbuf, ret, s2, r2, lambda i: plan.get(i, lambda: None)())
     for r in range(row_tiles):
         fg[r * TILE:(r + 1) * TILE, :] = dot(AT[r], gb[...])
-    finish_weight()
 
     pltpu.make_async_copy(hubret, hubret, rh2).wait()
     hub_sum = hubret_send[g].astype(F32)
@@ -372,6 +338,7 @@
     for e in reversed(range(halves)):
         at = landed(ret, r2, e)
         fg[...] = fg[...] + dot(ohT[:, at], ret[at, :])
+    finish_weight()
 
     flat = pl.ds(0, (nb - 1) * slots)
     drop = ret.at[flat]
@@ -379,11 +346,10 @@
     pltpu.make_async_copy(drop, drop, s2).wait()
     pltpu.make_async_copy(hubret, hubret, sh1).wait()
     pltpu.make_async_copy(hubret, hubret, sh2).wait()
-    pltpu.make_async_copy(ybuf, ybuf, ar_s.at[0]).wait()
-    pltpu.make_async_copy(xbuf, xbuf, ar_s.at[1]).wait()
-    pltpu.make_async_copy(zbuf.at[pl.ds(0, nz - 1)], zbuf.at[pl.ds(0, nz - 1)], ar_s.at[2]).wait()
-    pltpu.make_async_copy(xbuf, xbuf, ar_s.at[3]).wait()
-    pltpu.make_async_copy(wbuf.at[pl.ds(0, ng - 1)], wbuf.at[pl.ds(0, ng - 1)], ar_s.at[4]).wait()
+    others = zbuf.at[pl.ds(0, nz - 1)]
+    pltpu.make_async_copy(xbuf, xbuf, ar_s.at[0]).wait()
+    pltpu.make_async_copy(others, others, ar_s.at[1]).wait()
+    pltpu.make_async_copy(xbuf, xbuf, ar_s.at[2]).wait()
 
 
 def hand_out(a, b, c, a_out, b_out, c_out, sems):
@@ -408,7 +374,8 @@
     row_tiles = rows // TILE
     src_tiles = row_tiles + chunks + ng
     idx_rows = (chunks + 8) // 8 * 8
-    blocks = (TILE // ng // 8) * (fout // TILE) // inner
+    members = ng * inner
+    blocks = (fin // 8) * (fout // TILE) // members
     vm = pltpu.VMEM
     dma = pltpu.SemaphoreType.DMA
     scratch = [
@@ -425,10 +392,9 @@
         vm((rows, fin), F32), vm((rows, fin), BF16), vm((rows, fout), BF16), vm((rows, fin), BF16),
         vm((2, nz, TILE, fin), BF16), vm((nb * slots, fin), BF16),
         vm((ng, TILE, fin), BF16), vm((ng - 1, TILE, fin), BF16),
-        vm((fin, fout), F32), vm((ng - 1, TILE // ng, fout), F32), vm((inner, blocks, 8, TILE), F32),
-        vm((inner - 1, blocks, 8, TILE), F32), vm((nz, blocks, 8, TILE), F32), vm((blocks, 8, TILE), F32),
-        vm((inner, blocks, 8, TILE), F32), vm((ng, inner, blocks, 8, TILE), F32),
-        dma((9,)), dma, dma((2,)), dma, dma, dma, dma((2,)), dma, dma, dma((5,)), dma((5,)), dma,
+        vm((fin, fout), F32), vm((members, blocks, 8, TILE), F32), vm((members - 1, blocks, 8, TILE), F32),
+        vm((nz, blocks, 8, TILE), F32), vm((blocks, 8, TILE), F32), vm((members, blocks, 8, TILE), F32),
+        dma((9,)), dma, dma((2,)), dma, dma, dma, dma((2,)), dma, dma, dma((3,)), dma((3,)), dma,
     ]
     flops = 2 * (2 * rows * src_tiles * TILE * fin + 2 * rows * chunks * TILE * fin + 3 * rows * fin * fout)
     results = pl.pallas_call(

time: 53.4 us -> 47.3 us (0.89)
  Pallas kernels: 52.7 us -> 46.6 us
    pallas_call x1, Pallas kernels: 51.8 us -> 45.7 us  [body(): pl.pallas_call(functools.partial(kernel, nb, ng, inner), out_shape=[vm((r...]
where the time goes in v3:
time: 47.3 us; the launch traced here: 47.2 us
  Pallas kernels  46.6 us (99%)
  between operations  0.64 us (1%)
    pallas_call x1, Pallas kernels, body(): pl.pallas_call(functools.partial(kernel, nb, ng, inner), out_shape=[vm((r...  45.7 us

profile of v3, /device:TPU:1, one launch (start us, length us, event | category | flops | bytes accessed | tf_op | source)
XLA Modules:
  0.0 47.2 jit_solution(7974070253179641158)
XLA Ops:
  0.6 45.7 %shard_map.112 = (bf16[512,256]{1,0:T(8,128)(2,1)S(1)}, f32[128,256]{1,0:T(8,128)S(1)}, f32[512,128]{1,0:T(8,128)S(1)}) custom-call(bf16[512,128]{1,0:T(8,128)(2,1)} %feat_h.1, bf16[128,256]{1,0:T(8,128)(2,1)} %w_h.1, bf16[512,256]{1,0:T(8,128)(2,1)} %cot_h.1, bf16[64,128,128]{2,1,0:T(8,128)(2,1)} %tiles_h.1, s32[1,64]{1,0:T(1,128)} %bitcast.5, ...), custom_call_target="tpu_custom_call" | custom-call | flops 1442840576 | bytes 4194304 | tf_op jit(solution)/shard_map/pallas_call | solution.py:400
  46.4 0.9 %shard_map.113 = (bf16[512,256]{1,0:T(8,128)(2,1)}, f32[128,256]{1,0:T(8,128)}, f32[512,128]{1,0:T(8,128)}) custom-call(bf16[512,256]{1,0:T(8,128)(2,1)S(1)} %get-tuple-element.6.a, f32[128,256]{1,0:T(8,128)S(1)} %get-tuple-element.7.b, f32[512,128]{1,0:T(8,128)S(1)} %get-tuple-element.8.c), custom_call_target="tpu_custom_call" | custom-call | tf_op jit(solution)/shard_map/pallas_call | solution.py:414

commit v4 on v3

--- a/solution.py
+++ b/solution.py
@@ -73,8 +73,7 @@
         pl.semaphore_signal(barrier, inc=1, device_id=(z * inner + lax.rem(to, inner), to // inner), device_id_type=MESH)
         return 0
 
-    others = nb - inner + ng * inner - 1
-
+    greeted = nb - inner + ng * inner - 1
     lax.fori_loop(inner, nb, greet_z, 0)
     lax.fori_loop(1, ng * inner, greet_grp, 0)
 
@@ -104,7 +103,11 @@
         onehot = jnp.where(wide == lane_rows, 1.0, 0.0).astype(BF16)
         return dot(onehot, feat[...]).astype(BF16)
 
-    rounds = [(e, q) for e in reversed(range(halves)) for q in reversed(range(per_chunk))]
+    turns_back = range(per_chunk - 1, -1, -1)
+    few = nz // per_chunk if nz >= per_chunk else 1
+    firsts = [(m, min(m + few, nz)) for m in range(0, nz, few)]
+    rounds = [[(m, 1, q) for q in turns_back for m in range(*part_of)] for part_of in firsts]
+    rounds += [[(m, 0, q) for m in range(nz)] for q in turns_back]
 
     def to_z(m):
         step = (m + 1) // 2
@@ -115,24 +118,20 @@
 
     mine = pl.ds(pl.multiple_of(((half * nz + z) * per_chunk + lane_dev) * slots, slots), slots)
 
-    def exchange(buffer, landing, ssem, rsem, e, q):
-        piece = lax.rem(lane_dev + q, per_chunk)
-
-        def source(m):
-            return buffer.at[e, m, pl.ds(pl.multiple_of(piece * slots, slots), slots)]
-
-        def send(m, _):
-            pltpu.make_async_remote_copy(
-                src_ref=source(m), dst_ref=landing.at[mine], send_sem=ssem, recv_sem=rsem.at[e],
-                device_id=((to_z(m) * halves + to_half(e)) * per_chunk + piece, g), device_id_type=MESH,
-            ).start()
-            return 0
-
-        if e == 0 and q == 0:
-            lax.fori_loop(0, nz - 1, send, 0)
-            pltpu.make_async_copy(source(nz - 1), landing.at[mine], rsem.at[0]).start()
-        else:
-            lax.fori_loop(0, nz, send, 0)
+    far_first = [(nz // 2 + (m + 1) // 2 * (-1) ** m) % nz for m in range(nz)]
+    chunk_to = {(m, e): lax.rem(z + far_first[m], nz) * halves + to_half(e) for m in range(nz) for e in range(halves)}
+
+    def exchange(buffer, landing, ssem, rsem, some):
+        for m, e, q in some:
+            piece = lax.rem(lane_dev + q, per_chunk)
+            source = buffer.at[e, m, pl.ds(pl.multiple_of(piece * slots, slots), slots)]
+            if (m, e, q) == (nz - 1, 0, 0):
+                pltpu.make_async_copy(source, landing.at[mine], rsem.at[0]).start()
+            else:
+                pltpu.make_async_remote_copy(
+                    src_ref=source, dst_ref=landing.at[mine], send_sem=ssem, recv_sem=rsem.at[e],
+                    device_id=(chunk_to[m, e] * per_chunk + piece, g), device_id_type=MESH,
+                ).start()
 
     def landed(landing, rsem, e):
         some = landing.at[pl.ds(0, span)]
@@ -148,23 +147,28 @@
 
     hubsend[...] = gather(idxm[chunks:chunks + 1, :])
     hubs[g] = hubsend[...]
-    gather_some(halves - 1, 0, nz)
-    pl.semaphore_wait(barrier, others)
+    early = 4
+    for part_of in firsts[:early]:
+        gather_some(1, *part_of)
+    pl.semaphore_wait(barrier, greeted)
     for k in range(1, ng):
         pltpu.make_async_remote_copy(
             src_ref=hubsend, dst_ref=hubs.at[g], send_sem=sh1, recv_sem=rh1,
             device_id=(b, lax.rem(g + k, ng)), device_id_type=MESH,
         ).start()
 
-    def turns(produce, buffer, landing, ssem, rsem, between):
-        for i, (e, q) in enumerate(rounds):
-            exchange(buffer, landing, ssem, rsem, e, q)
-            turn = i % per_chunk
-            if e > 0:
-                produce(e - 1, turn * nz // per_chunk, (turn + 1) * nz // per_chunk)
+    def turns(produce, ready, buffer, landing, ssem, rsem, between):
+        for i, some in enumerate(rounds):
+            if i < len(firsts):
+                if i >= ready:
+                    produce(1, *firsts[i])
+                exchange(buffer, landing, ssem, rsem, some)
+                produce(0, *firsts[i])
+            else:
+                exchange(buffer, landing, ssem, rsem, some)
             between(i)
 
-    turns(gather_some, sendbuf, incoming, s1, r1, lambda i: None)
+    turns(gather_some, early, sendbuf, incoming, s1, r1, lambda i: None)
 
     loads[4].wait()
     loads[5].wait()
@@ -322,9 +326,8 @@
                 device_id=(b, to), device_id_type=MESH,
             ).start()
 
-    plan = {0: back_hubs, 2: over_z, 5: back_plane}
-    back_some(halves - 1, 0, nz)
-    turns(back_some, retbuf, ret, s2, r2, lambda i: plan.get(i, lambda: None)())
+    plan = {1: back_hubs, 3: over_z, 6: back_plane}
+    turns(back_some, 0, retbuf, ret, s2, r2, lambda i: plan.get(i, lambda: None)())
     for r in range(row_tiles):
         fg[r * TILE:(r + 1) * TILE, :] = dot(AT[r], gb[...])
 

time: 47.3 us -> 46.3 us (0.979)
  Pallas kernels: 46.6 us -> 45.6 us
    pallas_call x1, Pallas kernels: 45.7 us -> 44.7 us  [body(): pl.pallas_call(functools.partial(kernel, nb, ng, inner), out_shape=[vm((r...]
where the time goes in v4:
time: 46.3 us; the launch traced here: 46.2 us
  Pallas kernels  45.6 us (98%)
  between operations  0.64 us (1%)
    pallas_call x1, Pallas kernels, body(): pl.pallas_call(functools.partial(kernel, nb, ng, inner), out_shape=[vm((r...  44.7 us

profile of v4, /device:TPU:1, one launch (start us, length us, event | category | flops | bytes accessed | tf_op | source)
XLA Modules:
  0.0 46.2 jit_solution(12662302440599473579)
XLA Ops:
  0.6 44.7 %shard_map.112 = (bf16[512,256]{1,0:T(8,128)(2,1)S(1)}, f32[128,256]{1,0:T(8,128)S(1)}, f32[512,128]{1,0:T(8,128)S(1)}) custom-call(bf16[512,128]{1,0:T(8,128)(2,1)} %feat_h.1, bf16[128,256]{1,0:T(8,128)(2,1)} %w_h.1, bf16[512,256]{1,0:T(8,128)(2,1)} %cot_h.1, bf16[64,128,128]{2,1,0:T(8,128)(2,1)} %tiles_h.1, s32[1,64]{1,0:T(1,128)} %bitcast.5, ...), custom_call_target="tpu_custom_call" | custom-call | flops 1442840576 | bytes 4194304 | tf_op jit(solution)/shard_map/pallas_call | solution.py:403
  45.4 0.9 %shard_map.113 = (bf16[512,256]{1,0:T(8,128)(2,1)}, f32[128,256]{1,0:T(8,128)}, f32[512,128]{1,0:T(8,128)}) custom-call(bf16[512,256]{1,0:T(8,128)(2,1)S(1)} %get-tuple-element.6.a, f32[128,256]{1,0:T(8,128)S(1)} %get-tuple-element.7.b, f32[512,128]{1,0:T(8,128)S(1)} %get-tuple-element.8.c), custom_call_target="tpu_custom_call" | custom-call | tf_op jit(solution)/shard_map/pallas_call | solution.py:417

commit v5 on v4

--- a/solution.py
+++ b/solution.py
@@ -58,7 +58,7 @@
         (tcol_h, tcol), (tiles_h, tiles), (w_h, w), (cot_h, cot),
     ]
     loads = [pltpu.make_async_copy(h, v, in_sems.at[i]) for i, (h, v) in enumerate(ins)]
-    for load in loads:
+    for load in loads[:4]:
         load.start()
 
     barrier = pltpu.get_barrier_semaphore()
@@ -76,6 +76,8 @@
     greeted = nb - inner + ng * inner - 1
     lax.fori_loop(inner, nb, greet_z, 0)
     lax.fori_loop(1, ng * inner, greet_grp, 0)
+    for load in loads[4:]:
+        load.start()
 
     loads[0].wait()
     loads[1].wait()

time: 46.3 us -> 46.1 us (level)
  no operation moved by 1% of the time
where the time goes in v5:
time: 46.1 us; the launch traced here: 46 us
  Pallas kernels  45.4 us (98%)
  between operations  0.64 us (1%)
    pallas_call x1, Pallas kernels, body(): pl.pallas_call(functools.partial(kernel, nb, ng, inner), out_shape=[vm((r...  44.5 us

profile of v5, /device:TPU:1, one launch (start us, length us, event | category | flops | bytes accessed | tf_op | source)
XLA Modules:
  0.0 46.0 jit_solution(6105001142781165088)
XLA Ops:
  0.6 44.5 %shard_map.112 = (bf16[512,256]{1,0:T(8,128)(2,1)S(1)}, f32[128,256]{1,0:T(8,128)S(1)}, f32[512,128]{1,0:T(8,128)S(1)}) custom-call(bf16[512,128]{1,0:T(8,128)(2,1)} %feat_h.1, bf16[128,256]{1,0:T(8,128)(2,1)} %w_h.1, bf16[512,256]{1,0:T(8,128)(2,1)} %cot_h.1, bf16[64,128,128]{2,1,0:T(8,128)(2,1)} %tiles_h.1, s32[1,64]{1,0:T(1,128)} %bitcast.5, ...), custom_call_target="tpu_custom_call" | custom-call | flops 1442840576 | bytes 4194304 | tf_op jit(solution)/shard_map/pallas_call | solution.py:405
  45.2 0.9 %shard_map.113 = (bf16[512,256]{1,0:T(8,128)(2,1)}, f32[128,256]{1,0:T(8,128)}, f32[512,128]{1,0:T(8,128)}) custom-call(bf16[512,256]{1,0:T(8,128)(2,1)S(1)} %get-tuple-element.6.a, f32[128,256]{1,0:T(8,128)S(1)} %get-tuple-element.7.b, f32[512,128]{1,0:T(8,128)S(1)} %get-tuple-element.8.c), custom_call_target="tpu_custom_call" | custom-call | tf_op jit(solution)/shard_map/pallas_call | solution.py:419
